TPU v7x, 128 devices: a whole 4x4x4 slice. The times are simulated.
128 devices in a mesh: slab: 32 (over z, x, core), sub: 4 (over y).
Axes of the slice: x: 4, y: 4, z: 4, core: 2. Of those that a mesh axis runs over, the one named last changes fastest.
Arguments:
- starts: float32 [32, 8, 2048, 128], P('slab', 'sub'), may hold values from -6 to 6
- sources: bfloat16 [32, 8, 2048, 128], P('slab', 'sub'), may hold values from -6 to 6
- inverse_conductance: bfloat16 [8, 2048, 2048], P('sub'), as said below
- coarse_decay: float32 [32, 8, 2048], P('slab', 'sub'), as said below
- interface_nodes: int32 [8, 256], P('sub'), may hold values from 0 to 2047, as said below
- retire: int32 [128], replicated, may hold values from 0 to 2, as said below
Outputs:
- window: float32 [32, 8, 2048, 128], P('slab', 'sub')
Inputs may be any that keep to these rules, and one draw needn't show every extreme that they name: `interface_nodes`: within each subnetwork the interface nodes are distinct, and 0 and 2047 are in every subnetwork's list. `retire`: some case retires no slab and some retires 2. `coarse_decay`: entries lie in (0, 1]. `inverse_conductance`: each matrix has a positive diagonal.
All inputs are finite; a program needn't handle non-finite values.
Results may differ from a plain program's by a relative error of at most 0.0042.
Values sent between devices are 32-bit elements; how exact they have to be, the bound alone decides.
A program may use at most 192 MiB of HBM per device.

v0:
```python
import jax
import jax.numpy as jnp
from jax import lax
from jax.sharding import PartitionSpec as P

GRID_SUBNETWORKS = 8
STEPS = 8


def prefix(shard, axis, combine, identity):
    count, index = (lax.axis_size(axis), lax.axis_index(axis))
    everything = jax.tree.map(lambda part: lax.all_gather(part, axis), shard)
    start = jax.tree.map(
        lambda part, zero: jnp.broadcast_to(jnp.asarray(zero, part.dtype), part.shape),
        shard,
        identity,
    )

    def turn(k, before):
        reached = k < index
        new = combine(before, jax.tree.map(lambda part: part[k], everything))
        return jax.tree.map(lambda a, b: jnp.where(reached, a, b), new, before)

    return lax.fori_loop(0, count, turn, start)


def shifted(value, axis, steps):
    count = lax.axis_size(axis)
    first, last = (max(0, -steps), min(count, count - steps))
    return lax.ppermute(value, axis, [(source, source + steps) for source in range(first, last)])


def chain_combine(earlier, later):
    decay_early, offset_early = earlier
    decay_late, offset_late = later
    return (decay_late * decay_early, decay_late[..., None] * offset_early + offset_late)


def fine_slab(start, source, inverse_conductance, interface_nodes):
    state = start
    source_f = source.astype(jnp.float32)
    for step in range(STEPS):
        stepped = (state + source_f).astype(jnp.bfloat16)
        products = jnp.einsum(
            "snm,smc->snc", inverse_conductance, stepped, preferred_element_type=jnp.float32
        )
        rows = jnp.take_along_axis(products, interface_nodes[:, :, None], axis=1)
        local_total = jnp.sum(rows, axis=0)
        mean_iface = lax.psum(local_total, "sub") / GRID_SUBNETWORKS
        state = jax.vmap(lambda block, where_at: block.at[where_at].set(mean_iface))(
            products, interface_nodes
        )
    return state


def body(starts, sources, inverse_conductance, coarse_decay, interface_nodes, retire):
    start = starts[0]
    decay = coarse_decay[0]
    fine = fine_slab(start, sources[0], inverse_conductance, interface_nodes)
    correction = fine - decay[..., None] * start
    position = lax.axis_index("slab")
    leading = position == 0
    pair_decay = jnp.where(leading, jnp.zeros_like(decay), decay)
    pair_offset = jnp.where(leading, fine, correction)
    identity = (jnp.ones_like(decay), jnp.zeros_like(correction))
    composed_decay, composed_offset = prefix(
        (pair_decay, pair_offset), "slab", chain_combine, identity
    )
    current = composed_decay[..., None] * start + composed_offset
    slab_count = lax.axis_size("slab")
    most_retired = max(2, slab_count // 16)
    next_state = decay[..., None] * current + correction
    not_last = position < slab_count - 1

    def one_hop(turn, carried):
        moved = shifted(carried, "slab", -1)
        taken = jnp.logical_and(turn < retire - 1, not_last)
        return jnp.where(taken[None, None, :], moved, carried)

    held = lax.fori_loop(0, most_retired - 1, one_hop, next_state)
    result = jnp.where((retire == 0)[None, None, :], current, held)
    return result[None]


def solution(mesh):
    return jax.shard_map(
        body,
        mesh=mesh,
        in_specs=(
            P("slab", "sub", None, None),
            P("slab", "sub", None, None),
            P("sub", None, None),
            P("slab", "sub", None),
            P("sub", None),
            P(),
        ),
        out_specs=P("slab", "sub", None, None),
        check_vma=False,
    )
```

profile of v0, /device:TPU:7, one launch (start us, length us, event | category | flops | bytes accessed | tf_op | source)
XLA Modules:
  0.0 1020.4 jit_solution(18087139182001543871)
XLA Ops:
  7.9 13.7 %convolution_bitcast_fusion.7 = f32[2,2048,128]{1,2,0:T(8,128)} fusion(bf16[2,2048,2048]{2,1,0:T(8,128)(2,1)} %param.12, f32[1,2,2048,128]{3,2,1,0:T(8,128)} %param.10, bf16[1,2,2048,128]{3,2,1,0:T(8,128)(2,1)} %param.11), kind=kOutput, calls=%fused_computation.35 | convolution fusion | flops 2149056512 | bytes 22020096 | tf_op jit(solution)/shard_map/snm,smc->snc/dot_general | solution.py:44
  23.5 3.7 gather_fusion
  28.1 41.5 %all-reduce.9.cloned.1.call-done = f32[256,128]{1,0:T(8,128)} async-done(((f32[256,128]{1,0:T(8,128)}), f32[256,128]{1,0:T(8,128)}) %all-reduce.9.cloned.1.call-update) | async-done | bytes 131088 | tf_op jit(solution)/shard_map/psum | solution.py:49
  70.6 24.0 %scatter_fusion = f32[2,2048,128]{2,1,0:T(8,128)S(1)} fusion(f32[2,2048,128]{2,1,0:T(8,128)S(1)} %copy.33, s32[512]{0:T(512)S(1)} %bitcast.131, f32[512,128]{1,0:T(8,128)S(1)} %bitcast.148), kind=kCustom, calls=%fused_computation.8 | custom fusion | bytes 790528 | tf_op jit(solution)/shard_map/vmap()/scatter | solution.py:50
  94.6 12.8 %convolution_bitcast_fusion.6 = f32[2,2048,128]{1,2,0:T(8,128)} fusion(bf16[2,2048,2048]{2,1,0:T(8,128)(2,1)} %param.12, f32[2,2048,128]{2,1,0:T(8,128)S(1)} %scatter_fusion, bf16[1,2,2048,128]{3,2,1,0:T(8,128)(2,1)S(1)} %copy-done), kind=kOutput, calls=%fused_computation.34 | convolution fusion | flops 2149056512 | bytes 22020096 | tf_op jit(solution)/shard_map/snm,smc->snc/dot_general | solution.py:44
  114.3 41.2 %all-reduce.11.cloned.1.call-done = f32[256,128]{1,0:T(8,128)} async-done(((f32[256,128]{1,0:T(8,128)}), f32[256,128]{1,0:T(8,128)}) %all-reduce.11.cloned.1.call-update) | async-done | bytes 131088 | tf_op jit(solution)/shard_map/psum | solution.py:49
  156.5 24.0 %scatter_fusion.1 = f32[2,2048,128]{2,1,0:T(8,128)S(1)} fusion(f32[2,2048,128]{2,1,0:T(8,128)S(1)} %copy.36, s32[512]{0:T(512)S(1)} %bitcast.132, f32[512,128]{1,0:T(8,128)S(1)} %bitcast.149), kind=kCustom, calls=%fused_computation.9 | custom fusion | bytes 790528 | tf_op jit(solution)/shard_map/vmap()/scatter | solution.py:50
  180.5 12.8 %convolution_bitcast_fusion.5 = f32[2,2048,128]{1,2,0:T(8,128)} fusion(bf16[2,2048,2048]{2,1,0:T(8,128)(2,1)} %param.12, f32[2,2048,128]{2,1,0:T(8,128)S(1)} %scatter_fusion.1, bf16[1,2,2048,128]{3,2,1,0:T(8,128)(2,1)S(1)} %copy-done), kind=kOutput, calls=%fused_computation.33 | convolution fusion | flops 2149056512 | bytes 22020096 | tf_op jit(solution)/shard_map/snm,smc->snc/dot_general | solution.py:44
  199.7 41.7 %all-reduce.13.cloned.1.call-done = f32[256,128]{1,0:T(8,128)} async-done(((f32[256,128]{1,0:T(8,128)}), f32[256,128]{1,0:T(8,128)}) %all-reduce.13.cloned.1.call-update) | async-done | bytes 131088 | tf_op jit(solution)/shard_map/psum | solution.py:49
  242.4 24.0 %scatter_fusion.2 = f32[2,2048,128]{2,1,0:T(8,128)S(1)} fusion(f32[2,2048,128]{2,1,0:T(8,128)S(1)} %copy.39, s32[512]{0:T(512)S(1)} %bitcast.133, f32[512,128]{1,0:T(8,128)S(1)} %bitcast.150), kind=kCustom, calls=%fused_computation.10 | custom fusion | bytes 790528 | tf_op jit(solution)/shard_map/vmap()/scatter | solution.py:50
  266.4 12.8 %convolution_bitcast_fusion.4 = f32[2,2048,128]{1,2,0:T(8,128)} fusion(bf16[2,2048,2048]{2,1,0:T(8,128)(2,1)} %param.12, f32[2,2048,128]{2,1,0:T(8,128)S(1)} %scatter_fusion.2, bf16[1,2,2048,128]{3,2,1,0:T(8,128)(2,1)S(1)} %copy-done), kind=kOutput, calls=%fused_computation.32 | convolution fusion | flops 2149056512 | bytes 22020096 | tf_op jit(solution)/shard_map/snm,smc->snc/dot_general | solution.py:44
  285.8 41.5 %all-reduce.15.cloned.1.call-done = f32[256,128]{1,0:T(8,128)} async-done(((f32[256,128]{1,0:T(8,128)}), f32[256,128]{1,0:T(8,128)}) %all-reduce.15.cloned.1.call-update) | async-done | bytes 131088 | tf_op jit(solution)/shard_map/psum | solution.py:49
  328.3 24.0 %scatter_fusion.3 = f32[2,2048,128]{2,1,0:T(8,128)S(1)} fusion(f32[2,2048,128]{2,1,0:T(8,128)S(1)} %copy.42, s32[512]{0:T(512)S(1)} %bitcast.134, f32[512,128]{1,0:T(8,128)S(1)} %bitcast.151), kind=kCustom, calls=%fused_computation.11 | custom fusion | bytes 790528 | tf_op jit(solution)/shard_map/vmap()/scatter | solution.py:50
  352.3 12.8 %convolution_bitcast_fusion.3 = f32[2,2048,128]{1,2,0:T(8,128)} fusion(bf16[2,2048,2048]{2,1,0:T(8,128)(2,1)} %param.12, f32[2,2048,128]{2,1,0:T(8,128)S(1)} %scatter_fusion.3, bf16[1,2,2048,128]{3,2,1,0:T(8,128)(2,1)S(1)} %copy-done), kind=kOutput, calls=%fused_computation.31 | convolution fusion | flops 2149056512 | bytes 22020096 | tf_op jit(solution)/shard_map/snm,smc->snc/dot_general | solution.py:44
  371.6 41.7 %all-reduce.17.cloned.1.call-done = f32[256,128]{1,0:T(8,128)} async-done(((f32[256,128]{1,0:T(8,128)}), f32[256,128]{1,0:T(8,128)}) %all-reduce.17.cloned.1.call-update) | async-done | bytes 131088 | tf_op jit(solution)/shard_map/psum | solution.py:49
  414.2 24.0 %scatter_fusion.4 = f32[2,2048,128]{2,1,0:T(8,128)S(1)} fusion(f32[2,2048,128]{2,1,0:T(8,128)S(1)} %copy.45, s32[512]{0:T(512)S(1)} %bitcast.135, f32[512,128]{1,0:T(8,128)S(1)} %bitcast.152), kind=kCustom, calls=%fused_computation.12 | custom fusion | bytes 790528 | tf_op jit(solution)/shard_map/vmap()/scatter | solution.py:50
  438.2 12.8 %convolution_bitcast_fusion.2 = f32[2,2048,128]{1,2,0:T(8,128)} fusion(bf16[2,2048,2048]{2,1,0:T(8,128)(2,1)} %param.12, f32[2,2048,128]{2,1,0:T(8,128)S(1)} %scatter_fusion.4, bf16[1,2,2048,128]{3,2,1,0:T(8,128)(2,1)S(1)} %copy-done), kind=kOutput, calls=%fused_computation.30 | convolution fusion | flops 2149056512 | bytes 22020096 | tf_op jit(solution)/shard_map/snm,smc->snc/dot_general | solution.py:44
  457.7 41.5 %all-reduce.19.cloned.1.call-done = f32[256,128]{1,0:T(8,128)} async-done(((f32[256,128]{1,0:T(8,128)}), f32[256,128]{1,0:T(8,128)}) %all-reduce.19.cloned.1.call-update) | async-done | bytes 131088 | tf_op jit(solution)/shard_map/psum | solution.py:49
  500.1 24.0 %scatter_fusion.5 = f32[2,2048,128]{2,1,0:T(8,128)S(1)} fusion(f32[2,2048,128]{2,1,0:T(8,128)S(1)} %copy.48, s32[512]{0:T(512)S(1)} %bitcast.136, f32[512,128]{1,0:T(8,128)S(1)} %bitcast.153), kind=kCustom, calls=%fused_computation.13 | custom fusion | bytes 790528 | tf_op jit(solution)/shard_map/vmap()/scatter | solution.py:50
  524.1 12.8 %convolution_bitcast_fusion.1 = f32[2,2048,128]{1,2,0:T(8,128)} fusion(bf16[2,2048,2048]{2,1,0:T(8,128)(2,1)} %param.12, f32[2,2048,128]{2,1,0:T(8,128)S(1)} %scatter_fusion.5, bf16[1,2,2048,128]{3,2,1,0:T(8,128)(2,1)S(1)} %copy-done), kind=kOutput, calls=%fused_computation.29 | convolution fusion | flops 2149056512 | bytes 22020096 | tf_op jit(solution)/shard_map/snm,smc->snc/dot_general | solution.py:44
  543.4 41.7 %all-reduce.21.cloned.1.call-done = f32[256,128]{1,0:T(8,128)} async-done(((f32[256,128]{1,0:T(8,128)}), f32[256,128]{1,0:T(8,128)}) %all-reduce.21.cloned.1.call-update) | async-done | bytes 131088 | tf_op jit(solution)/shard_map/psum | solution.py:49
  586.1 24.0 %scatter_fusion.6 = f32[2,2048,128]{2,1,0:T(8,128)S(1)} fusion(f32[2,2048,128]{2,1,0:T(8,128)S(1)} %copy.51, s32[512]{0:T(512)S(1)} %bitcast.137, f32[512,128]{1,0:T(8,128)S(1)} %bitcast.154), kind=kCustom, calls=%fused_computation.14 | custom fusion | bytes 790528 | tf_op jit(solution)/shard_map/vmap()/scatter | solution.py:50
  610.1 12.8 %convolution_bitcast_fusion = f32[2,2048,128]{1,2,0:T(8,128)} fusion(bf16[2,2048,2048]{2,1,0:T(8,128)(2,1)} %param.12, f32[2,2048,128]{2,1,0:T(8,128)S(1)} %scatter_fusion.6, bf16[1,2,2048,128]{3,2,1,0:T(8,128)(2,1)S(1)} %copy-done), kind=kOutput, calls=%fused_computation.28 | convolution fusion | flops 2149056512 | bytes 22020096 | tf_op jit(solution)/shard_map/snm,smc->snc/dot_general | solution.py:44
  629.6 41.4 %all-reduce.23.cloned.1.call-done = f32[256,128]{1,0:T(8,128)} async-done(((f32[256,128]{1,0:T(8,128)}), f32[256,128]{1,0:T(8,128)}) %all-reduce.23.cloned.1.call-update) | async-done | bytes 131088 | tf_op jit(solution)/shard_map/psum | solution.py:49
  672.0 24.0 %scatter_fusion.7 = f32[2,2048,128]{2,1,0:T(8,128)S(1)} fusion(f32[2,2048,128]{2,1,0:T(8,128)S(1)} %copy.54, s32[512]{0:T(512)S(1)} %bitcast.138, f32[512,128]{1,0:T(8,128)S(1)} %bitcast.147), kind=kCustom, calls=%fused_computation.15 | custom fusion | bytes 790528 | tf_op jit(solution)/shard_map/vmap()/scatter | solution.py:50
  696.0 3.7 fusion.11
  699.8 27.5 %all_gather.10 = f32[32,2,2048]{2,1,0:T(2,128)S(1)} all-gather(f32[1,2,2048]{2,1,0:T(2,128)S(1)} %broadcast_select_fusion), channel_id=1, replica_groups=mesh['slab'=32,'sub'=4] {'slab'}, dimensions={0}, use_global_device_ids=true | all-gather | bytes 540672 | tf_op jit(solution)/shard_map/all_gather | solution.py:12
  727.3 177.2 %all-gather.3.cloned.1.call-done = f32[64,2048,128]{2,1,0:T(8,128)} async-done(((f32[2,2048,128]{2,1,0:T(8,128)}), f32[64,2048,128]{2,1,0:T(8,128)}) %all-gather.3.cloned.1.call-update) | async-done | bytes 67108880 | tf_op jit(solution)/shard_map/all_gather | solution.py:12
  904.6 71.0 %while.10 = (s32[]{:T(128)}, f32[2,2048]{1,0:T(2,128)S(1)}, f32[2,2048,128]{2,1,0:T(8,128)S(1)}, s32[]{:T(128)}, f32[32,2,2048]{2,1,0:T(2,128)S(1)}, /*index=5*/f32[32,2,2048,128]{3,2,1,0:T(8,128)}, s32[]{:T(128)}, s32[]{:T(128)}) while((s32[]{:T(128)}, f32[2,2048]{1,0:T(2,128)S(1)}, f32[2,2048,128]{2,1,0:T(8,128)S(1)}, ...), condition=%wide.region_25.27_spmd.clone, body=%wide.region_24.0_spmd.clone.sunk | while | flops 2109444 | bytes 6373491 | solution.py:24
  975.6 3.8 multiply_add_fusion
  981.6 27.6 %collective-permute-done = f32[2,2048,128]{2,1,0:T(8,128)} collective-permute-done((f32[2,2048,128]{2,1,0:T(8,128)}, f32[2,2048,128]{2,1,0:T(8,128)}, u32[]{:S(2)}, u32[]{:S(2)}) %collective-permute-start) | collective-permute-done | bytes 2097184 | tf_op jit(solution)/shard_map/while/body/eval_jaxpr/ppermute | solution.py:30
  1009.2 4.2 select_bitcast_fusion
  (138 shorter events, 129.9 us)
Async XLA Ops:
  6.5 63.1 %all-reduce.9.cloned.1.call-start = ((), (), s32[]{:S(2)}) async-start(), calls=%async_computation | async-start | bytes 262144 | tf_op jit(solution)/shard_map/psum | solution.py:49
  28.0 127.5 %all-reduce.11.cloned.1.call-start = ((), (), s32[]{:S(2)}) async-start(), calls=%async_computation.1 | async-start | bytes 262144 | tf_op jit(solution)/shard_map/psum | solution.py:49
  70.5 24.0 %copy-start = (bf16[1,2,2048,128]{3,2,1,0:T(8,128)(2,1)S(1)}, bf16[1,2,2048,128]{3,2,1,0:T(8,128)(2,1)}, u32[]{:S(2)}) copy-start(bf16[1,2,2048,128]{3,2,1,0:T(8,128)(2,1)} %param.11) | copy-start | bytes 3145732
  113.8 127.7 %all-reduce.13.cloned.1.call-start = ((), (), s32[]{:S(2)}) async-start(), calls=%async_computation.2 | async-start | bytes 262144 | tf_op jit(solution)/shard_map/psum | solution.py:49
  199.7 127.7 %all-reduce.15.cloned.1.call-start = ((), (), s32[]{:S(2)}) async-start(), calls=%async_computation.3 | async-start | bytes 262144 | tf_op jit(solution)/shard_map/psum | solution.py:49
  285.6 127.7 %all-reduce.17.cloned.1.call-start = ((), (), s32[]{:S(2)}) async-start(), calls=%async_computation.4 | async-start | bytes 262144 | tf_op jit(solution)/shard_map/psum | solution.py:49
  371.5 127.7 %all-reduce.19.cloned.1.call-start = ((), (), s32[]{:S(2)}) async-start(), calls=%async_computation.5 | async-start | bytes 262144 | tf_op jit(solution)/shard_map/psum | solution.py:49
  457.4 127.7 %all-reduce.21.cloned.1.call-start = ((), (), s32[]{:S(2)}) async-start(), calls=%async_computation.6 | async-start | bytes 262144 | tf_op jit(solution)/shard_map/psum | solution.py:49
  543.3 127.7 %all-reduce.23.cloned.1.call-start = ((), (), s32[]{:S(2)}) async-start(), calls=%async_computation.7 | async-start | bytes 262144 | tf_op jit(solution)/shard_map/psum | solution.py:49
  629.3 275.3 %all-gather.3.cloned.1.call-start = ((), (), s32[]{:S(2)}) async-start(), calls=%async_computation.8 | async-start | bytes 69206016 | tf_op jit(solution)/shard_map/all_gather | solution.py:12
  672.0 24.0 %copy-start.2 = (f32[1,2,2048]{2,1,0:T(2,128)S(1)}, f32[1,2,2048]{2,1,0:T(2,128)}, u32[]{:S(2)}) copy-start(f32[1,2,2048]{2,1,0:T(2,128)} %param.13) | copy-start | bytes 49156
  696.0 3.8 copy-start.1
  975.6 6.0 copy-start.3
  979.4 29.8 %collective-permute-start = (f32[2,2048,128]{2,1,0:T(8,128)}, f32[2,2048,128]{2,1,0:T(8,128)}, u32[]{:S(2)}, u32[]{:S(2)}) collective-permute-start(f32[2,2048,128]{2,1,0:T(8,128)} %multiply_add_fusion), channel_id=1, source_target_pairs={{4,0},{8,4},{12,8},{16,12},{20,16},{24,20},{28,24},{32,28},{36,32}... | collective-permute-start | bytes 6291464 | tf_op jit(solution)/shard_map/while/body/eval_jaxpr/ppermute | solution.py:30
Sparse Core Ops, SparseCore 0:
  28.1 41.4 all-reduce.8
  113.9 41.5 all-reduce.10
  199.8 41.5 all-reduce.12
  285.7 41.5 all-reduce.14
  371.6 41.6 all-reduce.16
  457.6 41.5 all-reduce.18
  543.5 41.6 all-reduce.20
  629.4 41.5 all-reduce.22
  699.9 204.6 all-gather.2
where the time goes:
time: 1030 us; the launch traced here: 1020 us
  waiting for transfers between devices  537 us (52%)
  local copies, waits for them, and re-layouts  237 us (23%)
  matrix products  103 us (10%)
  other arithmetic  96.8 us (9%)
  blocking collectives  27.5 us (3%)
  between operations  14.1 us (1%)
    psum x8, waiting for transfers between devices, fine_slab(): mean_iface = lax.psum(local_total, 'sub') / GRID_SUBNETWORKS  332 us
    scatter x8, local copies, waits for them, and re-layouts, fine_slab(): block.at[where_at].set(mean_iface)  192 us
    all_gather x1, waiting for transfers between devices, prefix(): everything = jax.tree.map(lambda part: lax.all_gather(part, axis), shard)  177 us
    dot_general x8, matrix products, fine_slab(): jnp.einsum('snm,smc->snc', inverse_conductance, stepped, preferred_elemen...  103 us
    select_n x64, other arithmetic, turn(): return jax.tree.map(lambda a, b: jnp.where(reached, a, b), new, before)  70 us
    gather x8, local copies, waits for them, and re-layouts, fine_slab(): rows = jnp.take_along_axis(products, interface_nodes[:, :, None], axis=1)  29.3 us
    ppermute x1, waiting for transfers between devices, shifted(): lax.ppermute(value, axis, [(source, source + steps) for source in range(f...  27.6 us
    all_gather x1, blocking collectives, prefix(): everything = jax.tree.map(lambda part: lax.all_gather(part, axis), shard)  27.5 us
  transfers between devices with their start and end apart: 10, of which 10 were waited for; matrix products, arithmetic and copies ran while one was open for 0% of the time, Pallas kernels for 0%

commit v1 on v0

v1 whole, which is shorter than its diff:
```python
import functools

import jax
import jax.numpy as jnp
from jax import lax
from jax.experimental import pallas as pl
from jax.experimental.pallas import tpu as pltpu
from jax.sharding import PartitionSpec as P

NODES = 2048
CASES = 128
IFACE = 256
STEPS = 8
SUBS = 8
SLABS = 32
CHIPS = SLABS // 2
PIECE = NODES // CHIPS
HALF = IFACE // 2
MESH = pl.DeviceIdType.MESH
F32, BF16 = jnp.float32, jnp.bfloat16


def dot(a, b):
    return jnp.dot(a, b, preferred_element_type=F32)


def split2(value):
    high = value.astype(BF16)
    return high, (value - high.astype(F32)).astype(BF16)


def block(index, size):
    return pl.ds(pl.multiple_of(index * size, size), size)


def column(row):
    return jnp.broadcast_to(row, (128, 128)).T


def kernel(
    dec_ref, idxc_ref, idxr_ref, ret_ref, starts_ref, sources_ref, cond_ref,
    out_ref,
    a, e, et, ai, ac, w, z, src, st, sbo, sbx, sf, rf, mask, dcol, dpk, decall,
    sI, bq, kh, kl, km, mh, ml, wI, tot,
    q, ra, h, rb, hb, rc, ss, rd,
    cc, cs, inbox, outbox, yb, c2, ws, rw, ob,
    lsem, asem, swsem, swrec, dsend, drecv,
    as_, ar_, bs_, br_, cs_, cr_, ds_, dr_,
    tis, tir, tos, tor, shs, shr, ws_, wr_,
):
    s, u = lax.axis_index("slab"), lax.axis_index("sub")
    c = lax.rem(s, 2)
    m = lax.div(s, 2)
    oc = 1 - c
    mate = (s + 1 - 2 * c, u)
    first = (s, u + 1 - 2 * lax.rem(u, 2))
    second = (s, 3 - u)

    loads = [
        pltpu.make_async_copy(cond_ref.at[c, pl.ds(i * 512, 512)], a.at[pl.ds(i * 512, 512)], asem.at[i])
        for i in range(4)
    ]
    load_sbx = pltpu.make_async_copy(sources_ref.at[oc], sbx, lsem.at[0])
    load_sbo = pltpu.make_async_copy(sources_ref.at[c], sbo, lsem.at[1])
    load_st = pltpu.make_async_copy(starts_ref.at[c], st.at[c], lsem.at[2])
    load_sbx.start()
    for load in loads:
        load.start()
    load_sbo.start()
    load_st.start()

    barrier = pltpu.get_barrier_semaphore()

    def greet(j, _):
        pl.semaphore_signal(barrier, inc=1, device_id=(lax.rem(s + j, SLABS), u), device_id_type=MESH)
        return 0

    lax.fori_loop(1, SLABS, greet, 0)
    pl.semaphore_signal(barrier, inc=1, device_id=first, device_id_type=MESH)
    pl.semaphore_signal(barrier, inc=1, device_id=second, device_id_type=MESH)
    pl.semaphore_wait(barrier, SLABS + 1)

    def remote(source, target, send, receive, to):
        return pltpu.make_async_remote_copy(
            src_ref=source, dst_ref=target, send_sem=send, recv_sem=receive,
            device_id=to, device_id_type=MESH,
        )

    swap_st = remote(starts_ref.at[oc], st.at[c], swsem.at[0], swrec.at[0], mate)
    swap_st.start()
    load_sbx.wait()
    sf[...] = sbx[...].astype(F32)
    swap_src = remote(sf, rf, swsem.at[1], swrec.at[1], mate)
    swap_src.start()

    def decay_out(j):
        t = lax.rem(s + j, SLABS)
        return remote(dec_ref.at[lax.rem(t, 2)], decall.at[s], dsend.at[j], drecv.at[s], (t, u))

    def decay_in(j):
        t = lax.rem(s + j, SLABS)
        return remote(dec_ref.at[c], decall.at[t], dsend.at[j], drecv.at[t], (t, u))

    def go(make):
        def one(j, _):
            make(j).start()
            return 0
        return one

    lax.fori_loop(1, SLABS, go(decay_out), 0)
    decall[s] = dec_ref[c]

    e[...] = (lax.broadcasted_iota(jnp.int32, (IFACE, NODES), 1) == idxc_ref[c]).astype(F32).astype(BF16)
    et[...] = (lax.broadcasted_iota(jnp.int32, (NODES, IFACE), 0) == idxr_ref[c]).astype(F32).astype(BF16)
    for load in loads:
        load.wait()

    def rows_of_interface(i, _):
        ai[:, block(i, 512)] = dot(e[...], a[:, block(i, 512)]).astype(BF16)
        return 0

    lax.fori_loop(0, 4, rows_of_interface, 0)
    aii = dot(ai[...], et[...])
    q[0, 0] = aii[:, :CASES]
    q[0, 1] = aii[:, CASES:]

    def ex_a(p):
        return remote(q.at[p, oc], ra.at[p], as_.at[p], ar_.at[p], mate)

    def ex_b(p):
        return [
            remote(h.at[p, pl.ds(0, HALF)], rb.at[p, pl.ds(0, HALF)], bs_.at[p, 0], br_.at[p, 0], first),
            remote(h.at[p, pl.ds(HALF, HALF)], rb.at[p, pl.ds(HALF, HALF)], bs_.at[p, 1], br_.at[p, 1], second),
        ]

    def ex_c(p):
        return [
            remote(hb.at[p, pl.ds(0, HALF)], rc.at[p, pl.ds(0, HALF)], cs_.at[p, 0], cr_.at[p, 0], second),
            remote(hb.at[p, pl.ds(HALF, HALF)], rc.at[p, pl.ds(HALF, HALF)], cs_.at[p, 1], cr_.at[p, 1], first),
        ]

    def ex_d(p):
        return remote(ss.at[p], rd.at[p], ds_.at[p], dr_.at[p], mate)

    def a_to_b(p):
        ex_a(p).wait()
        h[p] = q[p, c] + ra[p]
        for copy in ex_b(p):
            copy.start()

    def b_to_c(p):
        for copy in ex_b(p):
            copy.wait()
        hb[p] = h[p] + rb[p]
        for copy in ex_c(p):
            copy.start()

    def c_to_d(p):
        for copy in ex_c(p):
            copy.wait()
        ss[p] = hb[p] + rc[p]
        ex_d(p).start()

    def d_done(p):
        ex_d(p).wait()
        tot[c] = ss[p]
        tot[oc] = rd[p]

    ex_a(0).start()

    mask[...] = 1.0 - dot(et[...], jnp.ones((IFACE, CASES), BF16))
    a_to_b(0)

    def columns_of_interface(i, _):
        ac[block(i, 512), :] = dot(a[block(i, 512), :], et[...]).astype(BF16)
        return 0

    lax.fori_loop(0, 4, columns_of_interface, 0)

    load_sbo.wait()
    load_st.wait()
    swap_st.wait()
    swap_src.wait()
    src[c] = sbo[...]
    src[oc] = rf[...].astype(BF16)
    for j in range(2):
        w[0, :, j * CASES:(j + 1) * CASES] = (st[j] + src[j].astype(F32)).astype(BF16)
        sI[:, j * CASES:(j + 1) * CASES] = dot(e[...], src[j])
    bq[...] = dot(aii.astype(BF16), sI[...].astype(BF16))
    for ref in (kh, kl, mh, ml, wI):
        ref[...] = jnp.zeros_like(ref)

    def decay_wait(j, _):
        decay_out(j).wait_send()
        decay_in(j).wait_recv()
        return 0

    lax.fori_loop(1, SLABS, decay_wait, 0)
    b_to_c(0)

    def advance_mean():
        return km[...] + jnp.concatenate([tot[0], tot[1]], axis=1) * (1.0 / SUBS)

    def carry_mean():
        km[...] = dot(kh[...], mh[...]) + dot(kh[...], ml[...]) + dot(kl[...], mh[...])

    after = jnp.minimum(2 * m + 2, SLABS - 1)

    def step(k, _):
        p, pn = lax.rem(k, 2), lax.rem(k + 1, 2)
        qv = dot(ai[...], w[p]) + jnp.where(k > 0, 1.0, 0.0) * bq[...]
        q[pn, 0] = qv[:, :CASES]
        q[pn, 1] = qv[:, CASES:]
        ex_a(pn).start()
        carry_mean()
        for i in range(2):
            z[i * 512:(i + 1) * 512, :] = dot(a[i * 512:(i + 1) * 512, :], w[p])
        a_to_b(pn)
        for i in range(2):
            b = 2 * k + i
            dcol[0, block(b, 128), :] = column(decall[2 * m, pl.ds(b, 1), :])
            dcol[1, block(b, 128), :] = column(decall[2 * m + 1, pl.ds(b, 1), :])
            dcol[2, block(b, 128), :] = column(decall[after, pl.ds(b, 1), :])
            dpk[b] = column(decall[2 * b, pl.ds(m, 1), :] * decall[2 * b + 1, pl.ds(m, 1), :])
        c_to_d(p)
        for i in range(2, 4):
            z[i * 512:(i + 1) * 512, :] = dot(a[i * 512:(i + 1) * 512, :], w[p])
        d_done(p)

        @pl.when(k == 0)
        def _():
            high, low = split2(advance_mean())
            kh[...] = high
            kl[...] = low

        @pl.when(k > 0)
        def _():
            mean = advance_mean()
            high, low = split2(mean)
            mh[...] = high
            ml[...] = low
            wI[...] = (mean + sI[...]).astype(BF16)

        for i in range(4):
            rows = slice(i * 512, (i + 1) * 512)
            zf = z[rows, :] + dot(ac[rows, :], wI[...])
            z[rows, :] = zf
            for j in range(2):
                lanes = slice(j * CASES, (j + 1) * CASES)
                w[pn, rows, lanes] = (mask[rows, :] * (zf[:, lanes] + src[j, rows, :].astype(F32))).astype(BF16)
        b_to_c(pn)
        return 0

    lax.fori_loop(0, STEPS, step, 0)

    carry_mean()
    c_to_d(0)
    d_done(0)
    mean = advance_mean()
    m1, rest = mean.astype(BF16), mean - mean.astype(BF16).astype(F32)
    m2, m3 = split2(rest)
    kh[...] = m1
    kl[...] = m2
    mh[...] = m3

    def corrections(i, _):
        rows = block(i, 256)
        spread = dot(et[rows, :], kh[...]) + dot(et[rows, :], kl[...]) + dot(et[rows, :], mh[...])
        f0 = z[rows, :CASES] * mask[rows, :] + spread[:, :CASES]
        f1 = z[rows, CASES:] * mask[rows, :] + spread[:, CASES:]
        c0 = f0 - dcol[0, rows, :] * st[0, rows, :]
        c1 = f1 - dcol[1, rows, :] * st[1, rows, :]
        cc[0, rows, :] = c0
        cc[1, rows, :] = c1
        cs[rows, :] = dcol[1, rows, :] * jnp.where(m == 0, f0, c0) + c1
        return 0

    lax.fori_loop(0, NODES // 256, corrections, 0)

    def to_chip(o):
        t = lax.rem(m + o, CHIPS)
        return t, (2 * t + c, u)

    def in_out(o):
        t, there = to_chip(o)
        return remote(cs.at[block(t, PIECE)], inbox.at[m], tis.at[o], tir.at[m], there)

    def in_in(o):
        t, there = to_chip(o)
        return remote(cs.at[block(t, PIECE)], inbox.at[t], tis.at[o], tir.at[t], there)

    lax.fori_loop(1, CHIPS, go(in_out), 0)
    back = lax.rem(m + CHIPS - 1, CHIPS)
    shift = remote(cc.at[0], c2, shs, shr, (2 * back + c, u))
    shift.start()
    inbox[m] = cs[block(m, PIECE), :]

    def in_wait(o, _):
        in_out(o).wait_send()
        in_in(o).wait_recv()
        return 0

    lax.fori_loop(1, CHIPS, in_wait, 0)

    retire = ret_ref[...]

    def scan(k, state):
        new = dpk[k] * state + inbox[k]
        outbox[k] = jnp.where(retire >= 2, new, state)
        return new

    lax.fori_loop(0, CHIPS, scan, jnp.zeros((PIECE, CASES), F32))

    def back_out(o):
        t, there = to_chip(o)
        return remote(outbox.at[t], yb.at[block(m, PIECE)], tos.at[o], tor.at[m], there)

    def back_in(o):
        t, there = to_chip(o)
        return remote(outbox.at[t], yb.at[block(t, PIECE)], tos.at[o], tor.at[t], there)

    lax.fori_loop(1, CHIPS, go(back_out), 0)
    yb[block(m, PIECE), :] = outbox[m]
    shift.wait()

    def to_mate(j):
        rows = block(j, PIECE)
        return remote(ws.at[rows], rw.at[rows], ws_.at[j], wr_.at[j], mate)

    last = m == CHIPS - 1

    def finish(j):
        rows = block(j, PIECE)
        got = yb[rows, :]
        zero = jnp.logical_and(m == 0, retire < 2)
        got = jnp.where(zero, st[0, rows, :], got)
        v1 = dcol[0, rows, :] * got + cc[0, rows, :]
        v2 = dcol[1, rows, :] * v1 + cc[1, rows, :]
        v3 = jnp.where(last, got, dcol[2, rows, :] * got + c2[rows, :])
        w0 = jnp.where(retire == 1, v1, got)
        w1 = jnp.where(retire == 0, v1, jnp.where(retire == 1, v2, v3))
        ob[rows, :] = jnp.where(c == 0, w0, w1)
        ws[rows, :] = jnp.where(c == 0, w1, w0)
        to_mate(j).start()

    finish(m)

    def finish_at(o, _):
        t = lax.rem(m + CHIPS - o, CHIPS)
        back_in(CHIPS - o).wait_recv()
        finish(t)
        return 0

    lax.fori_loop(1, CHIPS, finish_at, 0)
    store_own = pltpu.make_async_copy(ob, out_ref.at[c], lsem.at[0])
    store_own.start()

    def last_waits(j, _):
        to_mate(j).wait()
        return 0

    lax.fori_loop(0, CHIPS, last_waits, 0)
    store_other = pltpu.make_async_copy(rw, out_ref.at[oc], lsem.at[1])
    store_other.start()

    def back_sent(o, _):
        back_out(o).wait_send()
        return 0

    lax.fori_loop(1, CHIPS, back_sent, 0)
    store_own.wait()
    store_other.wait()


def body(starts, sources, inverse_conductance, coarse_decay, interface_nodes, retire):
    hbm = pl.BlockSpec(memory_space=pl.ANY)
    vmem = pl.BlockSpec(memory_space=pltpu.VMEM)
    V, D = pltpu.VMEM, pltpu.SemaphoreType.DMA
    whole = (NODES, CASES)
    wide = (NODES, 2 * CASES)
    ifw = (IFACE, 2 * CASES)
    ex = (2, IFACE, CASES)
    scratch = [
        V((NODES, NODES), BF16), V((IFACE, NODES), BF16), V((NODES, IFACE), BF16),
        V((IFACE, NODES), BF16), V((NODES, IFACE), BF16),
        V((2,) + wide, BF16), V(wide, F32), V((2,) + whole, BF16), V((2,) + whole, F32),
        V(whole, BF16), V(whole, BF16), V(whole, F32), V(whole, F32), V(whole, F32),
        V((3,) + whole, F32), V((CHIPS, PIECE, CASES), F32), V((SLABS, 16, 128), F32),
        V(ifw, F32), V(ifw, F32), V((IFACE, IFACE), BF16), V((IFACE, IFACE), BF16), V(ifw, F32),
        V(ifw, BF16), V(ifw, BF16), V(ifw, BF16), V(ex, F32),
        V((2,) + ex, F32), V(ex, F32), V(ex, F32), V(ex, F32), V(ex, F32), V(ex, F32), V(ex, F32), V(ex, F32),
        V((2,) + whole, F32), V(whole, F32), V((CHIPS, PIECE, CASES), F32), V((CHIPS, PIECE, CASES), F32),
        V(whole, F32), V(whole, F32), V(whole, F32), V(whole, F32), V(whole, F32),
        D((3,)), D((4,)), D((2,)), D((2,)), D((SLABS,)), D((SLABS,)),
        D((2,)), D((2,)), D((2, 2)), D((2, 2)), D((2, 2)), D((2, 2)), D((2,)), D((2,)),
        D((CHIPS,)), D((CHIPS,)), D((CHIPS,)), D((CHIPS,)), D, D, D((CHIPS,)), D((CHIPS,)),
    ]
    out = pl.pallas_call(
        kernel,
        out_shape=jax.ShapeDtypeStruct((2,) + whole, F32),
        in_specs=[vmem] * 4 + [hbm] * 3,
        out_specs=hbm,
        scratch_shapes=scratch,
        compiler_params=pltpu.CompilerParams(
            collective_id=0, has_side_effects=True, vmem_limit_bytes=56 << 20
        ),
        cost_estimate=pl.CostEstimate(flops=2 * 9 * 2304 * 2304 * 256, bytes_accessed=16 << 20, transcendentals=0),
        name="parareal",
    )(
        coarse_decay.reshape(2, 16, 128),
        interface_nodes.reshape(2, IFACE, 1),
        interface_nodes.reshape(2, 1, IFACE),
        retire.reshape(1, CASES),
        starts[0],
        sources[0],
        inverse_conductance,
    )
    return out[None]


def solution(mesh):
    return jax.shard_map(
        body,
        mesh=mesh,
        in_specs=(
            P("slab", "sub", None, None),
            P("slab", "sub", None, None),
            P("sub", None, None),
            P("slab", "sub", None),
            P("sub", None),
            P(),
        ),
        out_specs=P("slab", "sub", None, None),
        check_vma=False,
    )
```

time: 1030 us -> 140 us (0.14)
  waiting for transfers between devices: 537 us -> 0 us
  local copies, waits for them, and re-layouts: 237 us -> 7.15 us
  Pallas kernels: 0 us -> 132 us
  matrix products: 103 us -> 0 us
  other arithmetic: 96.8 us -> 0 us
  blocking collectives: 27.5 us -> 0 us
  between operations: 14.1 us -> 0.01 us
    psum x8 -> x0, waiting for transfers between devices: 332 us -> none  [fine_slab(): mean_iface = lax.psum(local_total, 'sub') / GRID_SUBNETWORKS]
    scatter x8 -> x0, local copies, waits for them, and re-layouts: 192 us -> none  [fine_slab(): block.at[where_at].set(mean_iface)]
    all_gather x1 -> x0, waiting for transfers between devices: 177 us -> none  [prefix(): everything = jax.tree.map(lambda part: lax.all_gather(part, axis), shard)]
    pallas_call x0 -> x1, Pallas kernels: none -> 132 us  [body(): pl.pallas_call(kernel, out_shape=jax.ShapeDtypeStruct((2,) + whole, F32),...]
    dot_general x8 -> x0, matrix products: 103 us -> none  [fine_slab(): jnp.einsum('snm,smc->snc', inverse_conductance, stepped, preferred_elemen...]
    select_n x66 -> x0, other arithmetic: 73.8 us -> none  [the longest x64 70 us: turn(): return jax.tree.map(lambda a, b: jnp.where(reached, a, b), new, before)]
    gather x8 -> x0, local copies, waits for them, and re-layouts: 29.3 us -> none  [fine_slab(): rows = jnp.take_along_axis(products, interface_nodes[:, :, None], axis=1)]
    ppermute x1 -> x0, waiting for transfers between devices: 27.6 us -> none  [shifted(): lax.ppermute(value, axis, [(source, source + steps) for source in range(f...]
  transfers between devices with their start and end apart: 10 -> 0, of which waited for: 10 -> 0; matrix products, arithmetic and copies ran while one was open for 0% -> 0% of each run, Pallas kernels for 0% -> 0%
where the time goes in v1:
time: 140 us; the launch traced here: 139 us
  Pallas kernels  132 us (94%)
  local copies, waits for them, and re-layouts  7.15 us (5%)
    pallas_call x1, Pallas kernels, body(): pl.pallas_call(kernel, out_shape=jax.ShapeDtypeStruct((2,) + whole, F32),...  132 us
    unnamed x2, local copies, waits for them, and re-layouts  4.36 us

profile of v1, /device:TPU:7, one launch (start us, length us, event | category | flops | bytes accessed | tf_op | source)
XLA Modules:
  0.0 139.4 jit_solution(16041150905067365424)
XLA Ops:
  0.0 1.3 reshape.14.idxr_ref
  1.3 1.3 copy.10
  2.6 1.5 %copy.7.idxc_ref = s32[2,256,1]{2,1,0:T(8,128)} copy(s32[2,256,1]{1,0,2:T(2,128)} %bitcast.13) | data formatting | bytes 4096 | tf_op jit(solution)/shard_map/reshape | solution.py:411
  4.1 132.2 %parareal.1 = f32[2,2048,128]{2,1,0:T(8,128)} custom-call(f32[2,16,128]{2,1,0:T(8,128)} %bitcast.12, s32[2,256,1]{2,1,0:T(8,128)} %copy.7.idxc_ref, s32[2,1,256]{2,1,0:T(1,128)} %reshape.14.idxr_ref, s32[1,128]{1,0:T(1,128)} %bitcast.16, f32[2,2048,128]{2,1,0:T(8,128)} %bitcast.14, bf16[2,2048,128]{2,1,0:T(8,128)(2,1)} %bitcast.15, ...), custom_call_target="tpu_custom_call" | custom-call | flops 24461180928 | bytes 16777216 | tf_op jit(solution)/shard_map/parareal/pallas_call | solution.py:398
  136.4 3.0 %copy.12 = f32[1,2,2048,128]{3,2,1,0:T(8,128)} copy(f32[1,2,2048,128]{3,2,1,0:T(8,128)} %bitcast.10) | data formatting | bytes 4194304

commit v2 on v1

--- a/solution.py
+++ b/solution.py
@@ -16,6 +16,8 @@
 CHIPS = SLABS // 2
 PIECE = NODES // CHIPS
 HALF = IFACE // 2
+EARLY = 6
+SLOTS = 3
 MESH = pl.DeviceIdType.MESH
 F32, BF16 = jnp.float32, jnp.bfloat16
 
@@ -38,10 +40,10 @@
 
 
 def kernel(
-    dec_ref, idxc_ref, idxr_ref, ret_ref, starts_ref, sources_ref, cond_ref,
+    decay_ref, idx_ref, ret_ref, starts_ref, sources_ref, cond_ref,
     out_ref,
-    a, e, et, ai, ac, w, z, src, st, sbo, sbx, sf, rf, mask, dcol, dpk, decall,
-    sI, bq, kh, kl, km, mh, ml, wI, tot,
+    dec_ref, a, e, et, ai, ac, w, z, src, st, sbo, sbx, sf, rf, mask, dcol, dpk, decall,
+    sI, bq, gc, sg, k0h, k0l, k1h, k1l, m1h, m1l, m2h, m2l, tot,
     q, ra, h, rb, hb, rc, ss, rd,
     cc, cs, inbox, outbox, yb, c2, ws, rw, ob,
     lsem, asem, swsem, swrec, dsend, drecv,
@@ -78,6 +80,17 @@
     lax.fori_loop(1, SLABS, greet, 0)
     pl.semaphore_signal(barrier, inc=1, device_id=first, device_id_type=MESH)
     pl.semaphore_signal(barrier, inc=1, device_id=second, device_id_type=MESH)
+
+    for j in range(2):
+        for b in range(16):
+            dec_ref[j, b:b + 1, :] = decay_ref[j:j + 1, b * 128:(b + 1) * 128]
+    nodes_at = idx_ref[pl.ds(c, 1), :].astype(F32)
+    et[...] = (lax.broadcasted_iota(jnp.int32, (NODES, IFACE), 0).astype(F32) == nodes_at).astype(F32).astype(BF16)
+    lane = lax.broadcasted_iota(jnp.int32, (128, 128), 1).astype(F32)
+    for i in range(2):
+        nodes_down = column(nodes_at[:, i * 128:(i + 1) * 128])
+        for b in range(16):
+            e[i * 128:(i + 1) * 128, b * 128:(b + 1) * 128] = (lane + float(b * 128) == nodes_down).astype(F32).astype(BF16)
     pl.semaphore_wait(barrier, SLABS + 1)
 
     def remote(source, target, send, receive, to):
@@ -110,8 +123,6 @@
     lax.fori_loop(1, SLABS, go(decay_out), 0)
     decall[s] = dec_ref[c]
 
-    e[...] = (lax.broadcasted_iota(jnp.int32, (IFACE, NODES), 1) == idxc_ref[c]).astype(F32).astype(BF16)
-    et[...] = (lax.broadcasted_iota(jnp.int32, (NODES, IFACE), 0) == idxr_ref[c]).astype(F32).astype(BF16)
     for load in loads:
         load.wait()
 
@@ -169,13 +180,30 @@
     ex_a(0).start()
 
     mask[...] = 1.0 - dot(et[...], jnp.ones((IFACE, CASES), BF16))
+
+    def columns_of_interface(i, _):
+        rows = block(i, 512)
+        columns = dot(a[rows, :], et[...])
+        ac[rows, :] = columns.astype(BF16)
+        for j in range(2):
+            lanes = slice(j * CASES, (j + 1) * CASES)
+            w[1, rows, lanes] = (columns[:, lanes] * mask[rows, :]).astype(BF16)
+        return 0
+
+    lax.fori_loop(0, 4, columns_of_interface, 0)
     a_to_b(0)
-
-    def columns_of_interface(i, _):
-        ac[block(i, 512), :] = dot(a[block(i, 512), :], et[...]).astype(BF16)
-        return 0
-
-    lax.fori_loop(0, 4, columns_of_interface, 0)
+    kv = dot(ai[...], w[1])
+    q[1, 0] = kv[:, :CASES]
+    q[1, 1] = kv[:, CASES:]
+    ex_a(1).start()
+
+    def columns_twice(i, _):
+        rows = block(i, 512)
+        gc[rows, :] = dot(a[rows, :], w[1]).astype(BF16)
+        return 0
+
+    lax.fori_loop(0, 4, columns_twice, 0)
+    a_to_b(1)
 
     load_sbo.wait()
     load_st.wait()
@@ -187,7 +215,17 @@
         w[0, :, j * CASES:(j + 1) * CASES] = (st[j] + src[j].astype(F32)).astype(BF16)
         sI[:, j * CASES:(j + 1) * CASES] = dot(e[...], src[j])
     bq[...] = dot(aii.astype(BF16), sI[...].astype(BF16))
-    for ref in (kh, kl, mh, ml, wI):
+
+    def constant_source(i, _):
+        rows = block(i, 512)
+        fixed = dot(ac[rows, :], sI[...].astype(BF16))
+        for j in range(2):
+            lanes = slice(j * CASES, (j + 1) * CASES)
+            sg[j, rows, :] = fixed[:, lanes]
+        return 0
+
+    lax.fori_loop(0, 4, constant_source, 0)
+    for ref in (k0h, k0l, k1h, k1l, m1h, m1l, m2h, m2l):
         ref[...] = jnp.zeros_like(ref)
 
     def decay_wait(j, _):
@@ -198,74 +236,122 @@
     lax.fori_loop(1, SLABS, decay_wait, 0)
     b_to_c(0)
 
-    def advance_mean():
-        return km[...] + jnp.concatenate([tot[0], tot[1]], axis=1) * (1.0 / SUBS)
-
-    def carry_mean():
-        km[...] = dot(kh[...], mh[...]) + dot(kh[...], ml[...]) + dot(kl[...], mh[...])
+    def total():
+        return jnp.concatenate([tot[0], tot[1]], axis=1) * (1.0 / SUBS)
+
+    def next_mean():
+        mean = dot(k0h[...], m1h[...]) + dot(k0h[...], m1l[...]) + dot(k0l[...], m1h[...])
+        mean += dot(k1h[...], m2h[...]) + dot(k1h[...], m2l[...]) + dot(k1l[...], m2h[...])
+        return mean + total()
+
+    def push_mean():
+        mean = next_mean()
+        m2h[...] = m1h[...]
+        m2l[...] = m1l[...]
+        high, low = split2(mean)
+        m1h[...] = high
+        m1l[...] = low
+        return mean
 
     after = jnp.minimum(2 * m + 2, SLABS - 1)
 
     def step(k, _):
         p, pn = lax.rem(k, 2), lax.rem(k + 1, 2)
-        qv = dot(ai[...], w[p]) + jnp.where(k > 0, 1.0, 0.0) * bq[...]
-        q[pn, 0] = qv[:, :CASES]
-        q[pn, 1] = qv[:, CASES:]
-        ex_a(pn).start()
-        carry_mean()
-        for i in range(2):
+        now, next1, next2 = lax.rem(k, SLOTS), lax.rem(k + 1, SLOTS), lax.rem(k + 2, SLOTS)
+        later = jnp.where(k > 0, 1.0, 0.0)
+        qv = dot(ai[...], w[p]) + later * bq[...]
+        q[next2, 0] = qv[:, :CASES]
+        q[next2, 1] = qv[:, CASES:]
+        ex_a(next2).start()
+        def part(i):
             z[i * 512:(i + 1) * 512, :] = dot(a[i * 512:(i + 1) * 512, :], w[p])
-        a_to_b(pn)
+
+        part(0)
+        part(1)
+        a_to_b(next2)
+        b_to_c(next1)
+        c_to_d(now)
+        part(2)
         for i in range(2):
             b = 2 * k + i
             dcol[0, block(b, 128), :] = column(decall[2 * m, pl.ds(b, 1), :])
             dcol[1, block(b, 128), :] = column(decall[2 * m + 1, pl.ds(b, 1), :])
             dcol[2, block(b, 128), :] = column(decall[after, pl.ds(b, 1), :])
             dpk[b] = column(decall[2 * b, pl.ds(m, 1), :] * decall[2 * b + 1, pl.ds(m, 1), :])
-        c_to_d(p)
-        for i in range(2, 4):
-            z[i * 512:(i + 1) * 512, :] = dot(a[i * 512:(i + 1) * 512, :], w[p])
-        d_done(p)
+        part(3)
+        d_done(now)
 
         @pl.when(k == 0)
         def _():
-            high, low = split2(advance_mean())
-            kh[...] = high
-            kl[...] = low
-
-        @pl.when(k > 0)
+            high, low = split2(total())
+            k0h[...] = high
+            k0l[...] = low
+
+        @pl.when(k == 1)
         def _():
-            mean = advance_mean()
-            high, low = split2(mean)
-            mh[...] = high
-            ml[...] = low
-            wI[...] = (mean + sI[...]).astype(BF16)
+            high, low = split2(total())
+            k1h[...] = high
+            k1l[...] = low
+
+        @pl.when(k > 1)
+        def _():
+            push_mean()
 
         for i in range(4):
             rows = slice(i * 512, (i + 1) * 512)
-            zf = z[rows, :] + dot(ac[rows, :], wI[...])
-            z[rows, :] = zf
+            more = dot(gc[rows, :], m1h[...])
             for j in range(2):
                 lanes = slice(j * CASES, (j + 1) * CASES)
-                w[pn, rows, lanes] = (mask[rows, :] * (zf[:, lanes] + src[j, rows, :].astype(F32))).astype(BF16)
-        b_to_c(pn)
+                zf = z[rows, lanes] + more[:, lanes] + later * sg[j, rows, :]
+                z[rows, lanes] = zf
+                w[pn, rows, lanes] = (mask[rows, :] * (zf + src[j, rows, :].astype(F32))).astype(BF16)
         return 0
 
     lax.fori_loop(0, STEPS, step, 0)
 
-    carry_mean()
-    c_to_d(0)
-    d_done(0)
-    mean = advance_mean()
-    m1, rest = mean.astype(BF16), mean - mean.astype(BF16).astype(F32)
-    m2, m3 = split2(rest)
-    kh[...] = m1
-    kl[...] = m2
-    mh[...] = m3
-
-    def corrections(i, _):
-        rows = block(i, 256)
-        spread = dot(et[rows, :], kh[...]) + dot(et[rows, :], kl[...]) + dot(et[rows, :], mh[...])
+    now, next1 = STEPS % SLOTS, (STEPS + 1) % SLOTS
+    c_to_d(now)
+    b_to_c(next1)
+    d_done(now)
+    push_mean()
+
+    def last_columns(i, _):
+        rows = block(i, 512)
+        z[rows, :] += dot(ac[rows, :], m1h[...])
+        return 0
+
+    lax.fori_loop(0, 4, last_columns, 0)
+    c_to_d(next1)
+    d_done(next1)
+    mean = next_mean()
+    p1, rest = mean.astype(BF16), mean - mean.astype(BF16).astype(F32)
+    p2, p3 = split2(rest)
+    k0h[...] = p1
+    k0l[...] = p2
+    k1h[...] = p3
+
+    def to_chip(o):
+        t = lax.rem(m + o, CHIPS)
+        return t, (2 * t + c, u)
+
+    def in_out(o):
+        t, there = to_chip(o)
+        return remote(cs.at[block(t, PIECE)], inbox.at[m], tis.at[o], tir.at[m], there)
+
+    def in_in(o):
+        t, there = to_chip(o)
+        return remote(cs.at[block(t, PIECE)], inbox.at[t], tis.at[o], tir.at[t], there)
+
+    back = lax.rem(m + CHIPS - 1, CHIPS)
+
+    def shift(t):
+        rows = block(t, PIECE)
+        return remote(cc.at[0, rows], c2.at[rows], shs.at[t], shr.at[t], (2 * back + c, u))
+
+    def corrections(o, _):
+        t = lax.rem(m + o, CHIPS)
+        rows = block(t, PIECE)
+        spread = dot(et[rows, :], k0h[...]) + dot(et[rows, :], k0l[...]) + dot(et[rows, :], k1h[...])
         f0 = z[rows, :CASES] * mask[rows, :] + spread[:, :CASES]
         f1 = z[rows, CASES:] * mask[rows, :] + spread[:, CASES:]
         c0 = f0 - dcol[0, rows, :] * st[0, rows, :]
@@ -273,26 +359,18 @@
         cc[0, rows, :] = c0
         cc[1, rows, :] = c1
         cs[rows, :] = dcol[1, rows, :] * jnp.where(m == 0, f0, c0) + c1
-        return 0
-
-    lax.fori_loop(0, NODES // 256, corrections, 0)
-
-    def to_chip(o):
-        t = lax.rem(m + o, CHIPS)
-        return t, (2 * t + c, u)
-
-    def in_out(o):
-        t, there = to_chip(o)
-        return remote(cs.at[block(t, PIECE)], inbox.at[m], tis.at[o], tir.at[m], there)
-
-    def in_in(o):
-        t, there = to_chip(o)
-        return remote(cs.at[block(t, PIECE)], inbox.at[t], tis.at[o], tir.at[t], there)
-
-    lax.fori_loop(1, CHIPS, go(in_out), 0)
-    back = lax.rem(m + CHIPS - 1, CHIPS)
-    shift = remote(cc.at[0], c2, shs, shr, (2 * back + c, u))
-    shift.start()
+
+        @pl.when(o < CHIPS)
+        def _():
+            in_out(o).start()
+
+        @pl.when(jnp.logical_or(o <= EARLY, o == CHIPS))
+        def _():
+            shift(t).start()
+
+        return 0
+
+    lax.fori_loop(1, CHIPS + 1, corrections, 0)
     inbox[m] = cs[block(m, PIECE), :]
 
     def in_wait(o, _):
@@ -319,9 +397,17 @@
         t, there = to_chip(o)
         return remote(outbox.at[t], yb.at[block(t, PIECE)], tos.at[o], tor.at[t], there)
 
-    lax.fori_loop(1, CHIPS, go(back_out), 0)
+    def back_go(o, _):
+        back_out(o).start()
+
+        @pl.when(o < CHIPS - EARLY)
+        def _():
+            shift(lax.rem(m + CHIPS - o, CHIPS)).start()
+
+        return 0
+
+    lax.fori_loop(1, CHIPS, back_go, 0)
     yb[block(m, PIECE), :] = outbox[m]
-    shift.wait()
 
     def to_mate(j):
         rows = block(j, PIECE)
@@ -331,6 +417,7 @@
 
     def finish(j):
         rows = block(j, PIECE)
+        shift(j).wait_recv()
         got = yb[rows, :]
         zero = jnp.logical_and(m == 0, retire < 2)
         got = jnp.where(zero, st[0, rows, :], got)
@@ -357,6 +444,7 @@
 
     def last_waits(j, _):
         to_mate(j).wait()
+        shift(j).wait_send()
         return 0
 
     lax.fori_loop(0, CHIPS, last_waits, 0)
@@ -381,24 +469,24 @@
     ifw = (IFACE, 2 * CASES)
     ex = (2, IFACE, CASES)
     scratch = [
-        V((NODES, NODES), BF16), V((IFACE, NODES), BF16), V((NODES, IFACE), BF16),
+        V((2, 16, 128), F32), V((NODES, NODES), BF16), V((IFACE, NODES), BF16), V((NODES, IFACE), BF16),
         V((IFACE, NODES), BF16), V((NODES, IFACE), BF16),
         V((2,) + wide, BF16), V(wide, F32), V((2,) + whole, BF16), V((2,) + whole, F32),
         V(whole, BF16), V(whole, BF16), V(whole, F32), V(whole, F32), V(whole, F32),
         V((3,) + whole, F32), V((CHIPS, PIECE, CASES), F32), V((SLABS, 16, 128), F32),
-        V(ifw, F32), V(ifw, F32), V((IFACE, IFACE), BF16), V((IFACE, IFACE), BF16), V(ifw, F32),
-        V(ifw, BF16), V(ifw, BF16), V(ifw, BF16), V(ex, F32),
-        V((2,) + ex, F32), V(ex, F32), V(ex, F32), V(ex, F32), V(ex, F32), V(ex, F32), V(ex, F32), V(ex, F32),
+        V(ifw, F32), V(ifw, F32), V((NODES, IFACE), BF16), V((2,) + whole, F32),
+        *[V(ifw, BF16)] * 8, V(ex, F32),
+        V((SLOTS,) + ex, F32), *[V((SLOTS, IFACE, CASES), F32)] * 7,
         V((2,) + whole, F32), V(whole, F32), V((CHIPS, PIECE, CASES), F32), V((CHIPS, PIECE, CASES), F32),
         V(whole, F32), V(whole, F32), V(whole, F32), V(whole, F32), V(whole, F32),
         D((3,)), D((4,)), D((2,)), D((2,)), D((SLABS,)), D((SLABS,)),
-        D((2,)), D((2,)), D((2, 2)), D((2, 2)), D((2, 2)), D((2, 2)), D((2,)), D((2,)),
-        D((CHIPS,)), D((CHIPS,)), D((CHIPS,)), D((CHIPS,)), D, D, D((CHIPS,)), D((CHIPS,)),
+        D((SLOTS,)), D((SLOTS,)), *[D((SLOTS, 2))] * 4, D((SLOTS,)), D((SLOTS,)),
+        D((CHIPS,)), D((CHIPS,)), D((CHIPS,)), D((CHIPS,)), D((CHIPS,)), D((CHIPS,)), D((CHIPS,)), D((CHIPS,)),
     ]
     out = pl.pallas_call(
         kernel,
         out_shape=jax.ShapeDtypeStruct((2,) + whole, F32),
-        in_specs=[vmem] * 4 + [hbm] * 3,
+        in_specs=[vmem] * 3 + [hbm] * 3,
         out_specs=hbm,
         scratch_shapes=scratch,
         compiler_params=pltpu.CompilerParams(
@@ -407,9 +495,8 @@
         cost_estimate=pl.CostEstimate(flops=2 * 9 * 2304 * 2304 * 256, bytes_accessed=16 << 20, transcendentals=0),
         name="parareal",
     )(
-        coarse_decay.reshape(2, 16, 128),
-        interface_nodes.reshape(2, IFACE, 1),
-        interface_nodes.reshape(2, 1, IFACE),
+        coarse_decay[0],
+        interface_nodes,
         retire.reshape(1, CASES),
         starts[0],
         sources[0],

time: 140 us -> 127 us (0.907)
  Pallas kernels: 132 us -> 123 us
  local copies, waits for them, and re-layouts: 7.15 us -> 3.05 us
    pallas_call x1, Pallas kernels: 132 us -> 123 us  [body(): pl.pallas_call(kernel, out_shape=jax.ShapeDtypeStruct((2,) + whole, F32),...]
    reshape x2 -> x0, local copies, waits for them, and re-layouts: 2.79 us -> none  [the longest x1 1.53 us: body(): interface_nodes.reshape(2, IFACE, 1)]
    unnamed x2 -> x1, local copies, waits for them, and re-layouts: 4.36 us -> 3.05 us
where the time goes in v2:
time: 127 us; the launch traced here: 126 us
  Pallas kernels  123 us (97%)
  local copies, waits for them, and re-layouts  3.05 us (2%)
    pallas_call x1, Pallas kernels, body(): pl.pallas_call(kernel, out_shape=jax.ShapeDtypeStruct((2,) + whole, F32),...  123 us
    unnamed x1, local copies, waits for them, and re-layouts  3.05 us

profile of v2, /device:TPU:7, one launch (start us, length us, event | category | flops | bytes accessed | tf_op | source)
XLA Modules:
  0.0 126.2 jit_solution(816825792515277884)
XLA Ops:
  0.0 123.2 %parareal.1 = f32[2,2048,128]{2,1,0:T(8,128)} custom-call(f32[2,2048]{1,0:T(2,128)} %bitcast.8, s32[2,256]{1,0:T(2,128)} %idx_ref.1, s32[1,128]{1,0:T(1,128)} %bitcast.9, f32[2,2048,128]{2,1,0:T(8,128)} %bitcast.6, bf16[2,2048,128]{2,1,0:T(8,128)(2,1)} %bitcast.7, bf16[2,2048,2048]{2,1,0:T(8,128)(2,1)} %cond_ref.1), custom_call_target="tpu_custom_call" | custom-call | flops 24461180928 | bytes 16777216 | tf_op jit(solution)/shard_map/parareal/pallas_call | solution.py:486
  123.2 3.0 %copy.8 = f32[1,2,2048,128]{3,2,1,0:T(8,128)} copy(f32[1,2,2048,128]{3,2,1,0:T(8,128)} %bitcast.5) | data formatting | bytes 4194304

commit v3 on v2

--- a/solution.py
+++ b/solution.py
@@ -91,6 +91,11 @@
         nodes_down = column(nodes_at[:, i * 128:(i + 1) * 128])
         for b in range(16):
             e[i * 128:(i + 1) * 128, b * 128:(b + 1) * 128] = (lane + float(b * 128) == nodes_down).astype(F32).astype(BF16)
+
+    for load in loads:
+        load.wait()
+    for i in range(4):
+        ai[:, i * 512:(i + 1) * 512] = dot(e[...], a[:, i * 512:(i + 1) * 512]).astype(BF16)
     pl.semaphore_wait(barrier, SLABS + 1)
 
     def remote(source, target, send, receive, to):
@@ -123,14 +128,6 @@
     lax.fori_loop(1, SLABS, go(decay_out), 0)
     decall[s] = dec_ref[c]
 
-    for load in loads:
-        load.wait()
-
-    def rows_of_interface(i, _):
-        ai[:, block(i, 512)] = dot(e[...], a[:, block(i, 512)]).astype(BF16)
-        return 0
-
-    lax.fori_loop(0, 4, rows_of_interface, 0)
     aii = dot(ai[...], et[...])
     q[0, 0] = aii[:, :CASES]
     q[0, 1] = aii[:, CASES:]
@@ -182,7 +179,7 @@
     mask[...] = 1.0 - dot(et[...], jnp.ones((IFACE, CASES), BF16))
 
     def columns_of_interface(i, _):
-        rows = block(i, 512)
+        rows = slice(i * 512, (i + 1) * 512)
         columns = dot(a[rows, :], et[...])
         ac[rows, :] = columns.astype(BF16)
         for j in range(2):
@@ -190,7 +187,8 @@
             w[1, rows, lanes] = (columns[:, lanes] * mask[rows, :]).astype(BF16)
         return 0
 
-    lax.fori_loop(0, 4, columns_of_interface, 0)
+    for i in range(4):
+        columns_of_interface(i, 0)
     a_to_b(0)
     kv = dot(ai[...], w[1])
     q[1, 0] = kv[:, :CASES]
@@ -198,11 +196,12 @@
     ex_a(1).start()
 
     def columns_twice(i, _):
-        rows = block(i, 512)
+        rows = slice(i * 512, (i + 1) * 512)
         gc[rows, :] = dot(a[rows, :], w[1]).astype(BF16)
         return 0
 
-    lax.fori_loop(0, 4, columns_twice, 0)
+    for i in range(4):
+        columns_twice(i, 0)
     a_to_b(1)
 
     load_sbo.wait()
@@ -217,14 +216,15 @@
     bq[...] = dot(aii.astype(BF16), sI[...].astype(BF16))
 
     def constant_source(i, _):
-        rows = block(i, 512)
+        rows = slice(i * 512, (i + 1) * 512)
         fixed = dot(ac[rows, :], sI[...].astype(BF16))
         for j in range(2):
             lanes = slice(j * CASES, (j + 1) * CASES)
             sg[j, rows, :] = fixed[:, lanes]
         return 0
 
-    lax.fori_loop(0, 4, constant_source, 0)
+    for i in range(4):
+        constant_source(i, 0)
     for ref in (k0h, k0l, k1h, k1l, m1h, m1l, m2h, m2l):
         ref[...] = jnp.zeros_like(ref)
 
@@ -316,11 +316,12 @@
     push_mean()
 
     def last_columns(i, _):
-        rows = block(i, 512)
+        rows = slice(i * 512, (i + 1) * 512)
         z[rows, :] += dot(ac[rows, :], m1h[...])
         return 0
 
-    lax.fori_loop(0, 4, last_columns, 0)
+    for i in range(4):
+        last_columns(i, 0)
     c_to_d(next1)
     d_done(next1)
     mean = next_mean()

time: 127 us -> 125 us (0.984)
  no operation moved by 1% of the time
where the time goes in v3:
time: 125 us
  Pallas kernels  122 us (98%)
  local copies, waits for them, and re-layouts  3.05 us (2%)
    pallas_call x1, Pallas kernels, body(): pl.pallas_call(kernel, out_shape=jax.ShapeDtypeStruct((2,) + whole, F32),...  122 us
    unnamed x1, local copies, waits for them, and re-layouts  3.05 us

profile of v3, /device:TPU:7, one launch (start us, length us, event | category | flops | bytes accessed | tf_op | source)
XLA Modules:
  0.0 125.1 jit_solution(13815179019500062003)
XLA Ops:
  0.0 122.0 %parareal.1 = f32[2,2048,128]{2,1,0:T(8,128)} custom-call(f32[2,2048]{1,0:T(2,128)} %bitcast.8, s32[2,256]{1,0:T(2,128)} %idx_ref.1, s32[1,128]{1,0:T(1,128)} %bitcast.9, f32[2,2048,128]{2,1,0:T(8,128)} %bitcast.6, bf16[2,2048,128]{2,1,0:T(8,128)(2,1)} %bitcast.7, bf16[2,2048,2048]{2,1,0:T(8,128)(2,1)} %cond_ref.1), custom_call_target="tpu_custom_call" | custom-call | flops 24461180928 | bytes 16777216 | tf_op jit(solution)/shard_map/parareal/pallas_call | solution.py:487
  122.1 3.0 %copy.8 = f32[1,2,2048,128]{3,2,1,0:T(8,128)} copy(f32[1,2,2048,128]{3,2,1,0:T(8,128)} %bitcast.5) | data formatting | bytes 4194304

commit v4 on v3

--- a/solution.py
+++ b/solution.py
@@ -322,6 +322,15 @@
 
     for i in range(4):
         last_columns(i, 0)
+
+    def without_last_mean(i, _):
+        rows = block(i, 256)
+        for j in range(2):
+            lanes = slice(j * CASES, (j + 1) * CASES)
+            cc[j, rows, :] = z[rows, lanes] * mask[rows, :] - dcol[j, rows, :] * st[j, rows, :]
+        return 0
+
+    lax.fori_loop(0, NODES // 256, without_last_mean, 0)
     c_to_d(next1)
     d_done(next1)
     mean = next_mean()
@@ -353,10 +362,9 @@
         t = lax.rem(m + o, CHIPS)
         rows = block(t, PIECE)
         spread = dot(et[rows, :], k0h[...]) + dot(et[rows, :], k0l[...]) + dot(et[rows, :], k1h[...])
-        f0 = z[rows, :CASES] * mask[rows, :] + spread[:, :CASES]
-        f1 = z[rows, CASES:] * mask[rows, :] + spread[:, CASES:]
-        c0 = f0 - dcol[0, rows, :] * st[0, rows, :]
-        c1 = f1 - dcol[1, rows, :] * st[1, rows, :]
+        c0 = cc[0, rows, :] + spread[:, :CASES]
+        c1 = cc[1, rows, :] + spread[:, CASES:]
+        f0 = c0 + dcol[0, rows, :] * st[0, rows, :]
         cc[0, rows, :] = c0
         cc[1, rows, :] = c1
         cs[rows, :] = dcol[1, rows, :] * jnp.where(m == 0, f0, c0) + c1

time: 125 us -> 125 us (level)
  no operation moved by 1% of the time
where the time goes in v4:
time: 125 us
  Pallas kernels  122 us (98%)
  local copies, waits for them, and re-layouts  3.05 us (2%)
    pallas_call x1, Pallas kernels, body(): pl.pallas_call(kernel, out_shape=jax.ShapeDtypeStruct((2,) + whole, F32),...  122 us
    unnamed x1, local copies, waits for them, and re-layouts  3.05 us

profile of v4, /device:TPU:7, one launch (start us, length us, event | category | flops | bytes accessed | tf_op | source)
XLA Modules:
  0.0 125.1 jit_solution(1553254755789608486)
XLA Ops:
  0.0 122.0 %parareal.1 = f32[2,2048,128]{2,1,0:T(8,128)} custom-call(f32[2,2048]{1,0:T(2,128)} %bitcast.8, s32[2,256]{1,0:T(2,128)} %idx_ref.1, s32[1,128]{1,0:T(1,128)} %bitcast.9, f32[2,2048,128]{2,1,0:T(8,128)} %bitcast.6, bf16[2,2048,128]{2,1,0:T(8,128)(2,1)} %bitcast.7, bf16[2,2048,2048]{2,1,0:T(8,128)(2,1)} %cond_ref.1), custom_call_target="tpu_custom_call" | custom-call | flops 24461180928 | bytes 16777216 | tf_op jit(solution)/shard_map/parareal/pallas_call | solution.py:495
  122.1 3.0 %copy.8 = f32[1,2,2048,128]{3,2,1,0:T(8,128)} copy(f32[1,2,2048,128]{3,2,1,0:T(8,128)} %bitcast.5) | data formatting | bytes 4194304
